TPU v7x, 32 devices: a whole 2x2x4 slice. The times are simulated.
32 devices in a mesh: groups: 2 (over y), rep: 4 (over z), tp: 4 (over x, core).
Axes of the slice: x: 2, y: 2, z: 4, core: 2. Of those that a mesh axis runs over, the one named last changes fastest.
Arguments:
- row_states: bfloat16 [2, 64, 5120], P(None, ('groups', 'rep'), 'tp'), parts along dimension 1, may hold values from -6 to 6
- q_base: bfloat16 [2, 64, 8192], P(None, ('groups', 'rep'), 'tp'), parts along dimension 1, may hold values from -200 to 200
- cache_k: bfloat16 [2, 64, 384, 1024], P(None, ('groups', 'rep'), None, 'tp'), parts along dimension 1, may hold values from -8 to 8
- value_slots: bfloat16 [2, 64, 384, 1024], P(None, ('groups', 'rep'), None, 'tp'), parts along dimension 1, may hold values from -6 to 6
- current_key: bfloat16 [2, 64, 1024], P(None, ('groups', 'rep'), 'tp'), parts along dimension 1, may hold values from -6 to 6
- current_value: bfloat16 [2, 64, 1024], P(None, ('groups', 'rep'), 'tp'), parts along dimension 1, may hold values from -6 to 6
- cache_len: int32 [2, 64], P(None, ('groups', 'rep')), parts along dimension 1, may hold values from 2 to 384
- pool_a: bfloat16 [32, 32, 5120], P('rep', None, 'tp'), may hold values from -0.078125 to 0.078125
- pool_b: bfloat16 [32, 32, 8192], P('rep', None, 'tp'), may hold values from -1 to 1
- active_slots: int32 [2, 16], P(None, ('groups', 'rep')), parts along dimension 1, may hold values from 0 to 7, as said below
- row_adapter: int32 [2, 64, 1], P(None, ('groups', 'rep')), parts along dimension 1, may hold values from 0 to 7
Outputs:
- attended: bfloat16 [2, 64, 8192], P(None, ('groups', 'rep'), 'tp'), parts along dimension 1
There are 2 independent parts, one for each index of `groups`. A program takes and returns all parts, laid end to end along the dimension named above; an argument that names none is the same for every part. Nothing has to cross between parts.
Inputs may be any that keep to these rules, and one draw needn't show every extreme that they name: `active_slots`: within each micro-batch, the 2 entries of one owner name distinct local pages.
All inputs are finite; a program needn't handle non-finite values.
Results may differ from a plain program's by a relative error of at most 0.0058.
Values may be sent and summed in bfloat16 or wider, within the bound.
A program may use at most 64 MiB of HBM per device.

v0:
```python
import jax
import jax.numpy as jnp
from jax import lax
from jax.sharding import PartitionSpec as P

QUERY_HEADS = 64
KEY_VALUE_HEADS = 8
HEAD_SIZE = 128
R = 32
ROW_BATCHES = 2


def attend_rows(query_rows, key_slots, value_slot_cache, token_key, token_value, lengths):
    number_rows = query_rows.shape[0]
    slot_count = key_slots.shape[1]
    kv_local = key_slots.shape[2] // HEAD_SIZE
    heads_per_group = QUERY_HEADS // KEY_VALUE_HEADS
    score_scale = HEAD_SIZE ** (-0.5)
    query_head_rows = query_rows.reshape(number_rows, kv_local, heads_per_group, HEAD_SIZE)
    stored_keys = key_slots.reshape(number_rows, slot_count, kv_local, HEAD_SIZE)
    stored_values = value_slot_cache.reshape(number_rows, slot_count, kv_local, HEAD_SIZE)
    incoming_keys = token_key.reshape(number_rows, kv_local, HEAD_SIZE)
    incoming_values = token_value.reshape(number_rows, kv_local, HEAD_SIZE).astype(jnp.float32)
    scores = (
        jnp.einsum(
            "nhgd,nthd->nhgt", query_head_rows, stored_keys, preferred_element_type=jnp.float32
        )
        * score_scale
    )
    own_score = (
        jnp.einsum(
            "nhgd,nhd->nhg", query_head_rows, incoming_keys, preferred_element_type=jnp.float32
        )
        * score_scale
    )
    visible = jnp.arange(slot_count, dtype=jnp.int32)[None, :] < lengths[:, None]
    scores = jnp.where(visible[:, None, None, :], scores, -jnp.inf)
    highest = jnp.maximum(jnp.max(scores, axis=-1), own_score)
    weights = jnp.exp(scores - highest[..., None])
    own_weight = jnp.exp(own_score - highest)
    denominator = jnp.sum(weights, axis=-1) + own_weight
    own_low = own_weight.astype(jnp.bfloat16).astype(jnp.float32)
    mixed = jnp.einsum(
        "nhgt,nthd->nhgd",
        weights.astype(jnp.bfloat16),
        stored_values,
        preferred_element_type=jnp.float32,
    )
    mixed = mixed + own_low[..., None] * incoming_values[:, :, None, :]
    return (
        (mixed / denominator[..., None])
        .reshape(number_rows, kv_local * heads_per_group * HEAD_SIZE)
        .astype(jnp.bfloat16)
    )


def body(
    row_states,
    q_base,
    cache_k,
    value_slots,
    current_key,
    current_value,
    cache_len,
    pool_a,
    pool_b,
    active_slots,
    row_adapter,
):
    number_rows = row_states.shape[1]
    per_owner = active_slots.shape[1]
    active_count = per_owner * lax.axis_size("rep")
    query_width = q_base.shape[2]
    entries = jnp.arange(active_count, dtype=jnp.int32)
    outputs = []
    for step_index in range(ROW_BATCHES):
        states = row_states[step_index]
        chooser = (row_adapter[step_index] == entries[None, :]).astype(jnp.float32)
        owned_shrink = jnp.take(pool_a, active_slots[step_index], axis=0)
        owned_expand = jnp.take(pool_b, active_slots[step_index], axis=0)
        page_block = lax.all_gather(owned_shrink, "rep", axis=0, tiled=True)
        entries_here = page_block.shape[0]
        flat_pages = page_block.reshape(entries_here * R, page_block.shape[2])
        product = jnp.einsum(
            "nd,kd->nk", states, flat_pages, preferred_element_type=jnp.float32
        ).reshape(number_rows, entries_here, R)
        partial_value = jnp.sum(product * chooser[:, :, None], axis=1)
        shrink = lax.psum(partial_value, "tp").astype(jnp.bfloat16)
        expand_page_block = lax.all_gather(owned_expand, "rep", axis=0, tiled=True)
        expand_entries_here = expand_page_block.shape[0]
        expand_chosen = chooser.astype(jnp.bfloat16)
        spread = (expand_chosen[:, :, None] * shrink[:, None, :]).reshape(
            number_rows, expand_entries_here * R
        )
        expand_flat_pages = expand_page_block.reshape(expand_entries_here * R, query_width)
        delta_rows = jnp.dot(spread, expand_flat_pages, preferred_element_type=jnp.float32)
        query_rows = (q_base[step_index].astype(jnp.float32) + delta_rows).astype(jnp.bfloat16)
        outputs.append(
            attend_rows(
                query_rows,
                cache_k[step_index],
                value_slots[step_index],
                current_key[step_index],
                current_value[step_index],
                cache_len[step_index],
            )
        )
    return jnp.stack(outputs)


def solution(mesh):
    placed = (
        P(None, ("groups", "rep"), "tp"),
        P(None, ("groups", "rep"), "tp"),
        P(None, ("groups", "rep"), None, "tp"),
        P(None, ("groups", "rep"), None, "tp"),
        P(None, ("groups", "rep"), "tp"),
        P(None, ("groups", "rep"), "tp"),
        P(None, ("groups", "rep")),
        P("rep", None, "tp"),
        P("rep", None, "tp"),
        P(None, ("groups", "rep")),
        P(None, ("groups", "rep"), None),
    )
    return jax.shard_map(
        body,
        mesh=mesh,
        in_specs=placed,
        out_specs=P(None, ("groups", "rep"), "tp"),
        check_vma=False,
    )
```

profile of v0, /device:TPU:0, one launch (start us, length us, event | category | flops | bytes accessed | tf_op | source)
XLA Modules:
  0.0 96.7 jit_solution(3670286646606604165)
XLA Ops:
  6.5 0.8 compare_and_fusion.1
  7.4 0.4 copy-done
  7.8 0.6 gather_fusion.1
  8.4 0.8 broadcast_select_fusion.1
  9.2 0.0 all-gather.3.cloned.1.call-update
  9.2 0.0 all-gather.5.cloned.1.call-start
  9.3 0.6 gather_fusion.3
  9.8 0.0 copy-start.6
  9.9 0.8 broadcast_select_fusion
  10.7 0.0 all-gather.5.cloned.1.call-update
  10.7 0.6 gather_fusion.2
  11.3 0.6 gather_fusion
  11.9 0.1 iota_compare_fusion.1
  12.0 0.1 iota_compare_fusion
  12.0 0.1 copy.32
  12.1 0.1 copy.39
  12.2 0.1 broadcast_select_fusion.2
  12.3 0.1 broadcast_select_fusion.3
  12.4 26.4 %all_gather.12 = bf16[8,32,1280]{2,1,0:T(8,128)(2,1)S(1)} all-gather(bf16[2,32,1280]{2,1,0:T(8,128)(2,1)S(1)} %broadcast_select_fusion.3), channel_id=1, replica_groups=mesh['groups'=2,'rep'=4,'tp'=4] {'rep'}, dimensions={0}, use_global_device_ids=true | all-gather | bytes 819200 | tf_op jit(solution)/shard_map/all_gather | solution.py:81
  38.8 0.2 convolution_bitcast_fusion.3
  39.0 0.1 reshape.217
  39.1 20.9 %all_gather.14 = bf16[8,32,1280]{2,1,0:T(8,128)(2,1)S(1)} all-gather(bf16[2,32,1280]{2,1,0:T(8,128)(2,1)S(1)} %broadcast_select_fusion.2), channel_id=1, replica_groups=mesh['groups'=2,'rep'=4,'tp'=4] {'rep'}, dimensions={0}, use_global_device_ids=true | all-gather | bytes 819200 | tf_op jit(solution)/shard_map/all_gather | solution.py:81
  60.0 0.2 convolution_bitcast_fusion.2
  60.2 0.1 reshape.220
  60.3 0.0 copy-start.1
  60.3 3.6 %fusion.42 = (bf16[1,8,384,256]{3,2,1,0:T(8,128)(2,1)S(1)}, bf16[1,8,384,256]{3,2,1,0:T(8,128)(2,1)}) fusion(bf16[2,8,384,256]{3,2,1,0:T(8,128)(2,1)} %param.17), kind=kLoop, calls=%fused_computation.85 | loop fusion | bytes 6291456 | tf_op jit(solution)/shard_map/slice | solution.py:101
  63.9 0.0 copy-done.1
  63.9 2.0 %fusion.43 = (bf16[1,8,384,256]{3,2,1,0:T(8,128)(2,1)}, bf16[1,8,384,256]{3,2,1,0:T(8,128)(2,1)}) fusion(bf16[2,8,384,256]{3,2,1,0:T(8,128)(2,1)S(1)} %copy-done.1), kind=kLoop, calls=%fused_computation.86 | loop fusion | bytes 6291456 | tf_op jit(solution)/shard_map/slice | solution.py:102
  65.8 0.1 multiply_reduce_fusion
  66.0 1.6 %copy.54 = bf16[1,8,384,256]{2,3,1,0:T(8,128)(2,1)} copy(bf16[1,8,384,256]{3,2,1,0:T(8,128)(2,1)S(1)} %get-tuple-element.13) | data formatting | bytes 3145728
  67.5 1.9 %copy.56 = bf16[1,8,384,256]{2,3,1,0:T(8,128)(2,1)S(1)} copy(bf16[1,8,384,256]{3,2,1,0:T(8,128)(2,1)} %get-tuple-element.14) | data formatting | bytes 3145728
  69.4 2.6 %copy.55 = bf16[1,8,384,256]{2,3,1,0:T(8,128)(2,1)} copy(bf16[1,8,384,256]{3,2,1,0:T(8,128)(2,1)} %get-tuple-element.15) | data formatting | bytes 3145728
  72.0 2.6 %copy.57 = bf16[1,8,384,256]{2,3,1,0:T(8,128)(2,1)} copy(bf16[1,8,384,256]{3,2,1,0:T(8,128)(2,1)} %get-tuple-element.16) | data formatting | bytes 3145728
  74.7 6.1 %all-reduce = (bf16[8,32]{1,0:T(8,128)(2,1)S(1)}, bf16[8,32]{1,0:T(8,128)(2,1)S(1)}) all-reduce(f32[8,32]{1,0:T(8,128)S(1)} %get-tuple-element.39, f32[8,32]{1,0:T(8,128)S(1)} %get-tuple-element.40), channel_id=1, replica_groups=mesh['groups'=2,'rep'=4,'tp'=4] {'tp'}, use_global_device_ids=true, to_apply=%region_5.8 | all-reduce | flops 512 | bytes 3072 | tf_op jit(solution)/shard_map/psum | solution.py:88
  80.8 0.0 all-gather.3.cloned.1.call-done
  80.9 1.6 %fusion.2 = bf16[8,2048]{1,0:T(8,128)(2,1)S(1)} fusion(bf16[8,32,2048]{2,1,0:T(8,128)(2,1)} %all-gather.3.cloned.1.call-done, bf16[2,8,2048]{2,1,0:T(8,128)(2,1)S(1)} %copy-done.5, bf16[8,32]{1,0:T(8,128)(2,1)S(1)} %get-tuple-element.8, bf16[8,8]{0,1:T(8,128)(2,1)S(1)} %get-tuple-element.31), kind=kOutput, calls=%fused_computation.8 | convolution fusion | flops 8439808 | bytes 1114752 | tf_op jit(solution)/shard_map/dot_general | solution.py:96
  82.5 0.1 fusion.21
  82.6 1.9 %fusion.45 = (f32[8,2,8]{2,1,0:T(2,128)S(1)}, f32[8,2,8,384]{3,2,1,0:T(8,128)S(1)}) fusion(bf16[8,384,2,128]{1,3,2,0:T(8,128)(2,1)} %bitcast.81, bf16[8,2,8,128]{3,0,2,1:T(8,128)(2,1)S(1)} %bitcast.89, pred[8,384]{1,0:T(8,128)(4,1)S(1)} %iota_compare_fusion.1), kind=kOutput, calls=%fused_computation.88 | convolution fusion | flops 12730240 | bytes 1805824 | tf_op jit(solution)/shard_map/nhgd,nthd->nhgt/dot_general | solution.py:25
  84.5 0.2 fusion.10
  84.7 0.0 all-gather.5.cloned.1.call-done
  84.8 1.7 %fusion.3 = bf16[8,2048]{1,0:T(8,128)(2,1)S(1)} fusion(bf16[8,32,2048]{2,1,0:T(8,128)(2,1)} %all-gather.5.cloned.1.call-done, bf16[2,8,2048]{2,1,0:T(8,128)(2,1)S(1)} %copy-done.5, bf16[8,32]{1,0:T(8,128)(2,1)S(1)} %get-tuple-element.6, bf16[8,8]{0,1:T(8,128)(2,1)S(1)} %get-tuple-element.33), kind=kOutput, calls=%fused_computation.9 | convolution fusion | flops 8439808 | bytes 1114752 | tf_op jit(solution)/shard_map/dot_general | solution.py:96
  86.5 0.1 fusion.18
  86.6 0.5 fusion.44
  87.1 0.2 fusion.12
  87.4 0.7 fusion.8
  88.1 0.4 copy-done.2
  88.5 0.7 fusion.9
  89.3 0.6 pad_maximum_fusion
  (34 shorter events, 0.2 us)
Async XLA Ops:
  6.5 1.3 %copy-start = (bf16[8,32,2048]{2,1,0:T(8,128)(2,1)S(1)}, bf16[8,32,2048]{2,1,0:T(8,128)(2,1)}, u32[]{:S(2)}) copy-start(bf16[8,32,2048]{2,1,0:T(8,128)(2,1)} %param.23) | copy-start | bytes 3145732
  6.5 4.2 %copy-start.4 = (bf16[8,32,1280]{2,1,0:T(8,128)(2,1)S(1)}, bf16[8,32,1280]{2,1,0:T(8,128)(2,1)}, u32[]{:S(2)}) copy-start(bf16[8,32,1280]{2,1,0:T(8,128)(2,1)} %param.22) | copy-start | bytes 1966084
  6.5 74.3 %all-gather.3.cloned.1.call-start = ((), (), s32[]{:S(2)}) async-start(), calls=%async_computation | async-start | bytes 1310720 | tf_op jit(solution)/shard_map/all_gather | solution.py:89
  7.8 4.0 %copy-start.9 = (s32[2,8]{1,0:T(2,128)S(1)}, s32[2,8]{1,0:T(2,128)}, u32[]{:S(2)}) copy-start(s32[2,8]{1,0:T(2,128)} %param.21) | copy-start | bytes 196
  7.8 4.1 %copy-start.10 = (s32[2,8,1]{1,2,0:T(1,128)S(1)}, s32[2,8,1]{1,2,0:T(1,128)}, u32[]{:S(2)}) copy-start(s32[2,8,1]{1,2,0:T(1,128)} %param.25) | copy-start | bytes 196
  7.8 4.4 %copy-start.7 = (bf16[2,8,256]{2,1,0:T(8,128)(2,1)S(1)}, bf16[2,8,256]{2,1,0:T(8,128)(2,1)}, u32[]{:S(2)}) copy-start(bf16[2,8,256]{2,1,0:T(8,128)(2,1)} %param.20) | copy-start | bytes 24580
  9.2 75.5 %all-gather.5.cloned.1.call-start = ((), (), s32[]{:S(2)}) async-start(), calls=%async_computation.1 | async-start | bytes 1310720 | tf_op jit(solution)/shard_map/all_gather | solution.py:89
  9.8 28.9 %copy-start.6 = (bf16[2,8,1280]{2,1,0:T(8,128)(2,1)S(1)}, bf16[2,8,1280]{2,1,0:T(8,128)(2,1)}, u32[]{:S(2)}) copy-start(bf16[2,8,1280]{2,1,0:T(8,128)(2,1)} %param.15) | copy-start | bytes 122884
  60.3 3.6 %copy-start.1 = (bf16[2,8,384,256]{3,2,1,0:T(8,128)(2,1)S(1)}, bf16[2,8,384,256]{3,2,1,0:T(8,128)(2,1)}, u32[]{:S(2)}) copy-start(bf16[2,8,384,256]{3,2,1,0:T(8,128)(2,1)} %param.18) | copy-start | bytes 9437188
  72.0 8.8 %copy-start.8 = (bf16[2,8,256]{2,1,0:T(8,128)(2,1)S(1)}, bf16[2,8,256]{2,1,0:T(8,128)(2,1)}, u32[]{:S(2)}) copy-start(bf16[2,8,256]{2,1,0:T(8,128)(2,1)} %param.19) | copy-start | bytes 24580
  72.0 8.8 %copy-start.5 = (bf16[2,8,2048]{2,1,0:T(8,128)(2,1)S(1)}, bf16[2,8,2048]{2,1,0:T(8,128)(2,1)}, u32[]{:S(2)}) copy-start(bf16[2,8,2048]{2,1,0:T(8,128)(2,1)} %param.16) | copy-start | bytes 196612
  84.8 2.6 %copy-start.3 = (bf16[1,8,384,256]{2,3,1,0:T(8,128)(2,1)S(1)}, bf16[1,8,384,256]{2,3,1,0:T(8,128)(2,1)}, u32[]{:S(2)}) copy-start(bf16[1,8,384,256]{2,3,1,0:T(8,128)(2,1)} %copy.55) | copy-start | bytes 4718596
  87.1 1.4 %copy-start.2 = (bf16[1,8,384,256]{2,3,1,0:T(8,128)(2,1)S(1)}, bf16[1,8,384,256]{2,3,1,0:T(8,128)(2,1)}, u32[]{:S(2)}) copy-start(bf16[1,8,384,256]{2,3,1,0:T(8,128)(2,1)} %copy.57) | copy-start | bytes 4718596
Sparse Core Ops, SparseCore 0:
  9.3 42.2 all-gather.2
  53.2 28.0 all-gather.4
where the time goes:
time: 97.1 us; the launch traced here: 96.7 us
  blocking collectives  53.4 us (55%)
  local copies, waits for them, and re-layouts  17.8 us (18%)
  between operations  13.7 us (14%)
  matrix products  7.83 us (8%)
  other arithmetic  3.97 us (4%)
    all_gather x2, blocking collectives, body(): page_block = lax.all_gather(owned_shrink, 'rep', axis=0, tiled=True)  47.3 us
    unnamed x26, local copies, waits for them, and re-layouts  9.58 us
    psum x1, blocking collectives, body(): shrink = lax.psum(partial_value, 'tp').astype(jnp.bfloat16)  6.13 us
    slice x1, local copies, waits for them, and re-layouts, body(): cache_k[step_index]  3.57 us
    dot_general x2, matrix products, body(): jnp.dot(spread, expand_flat_pages, preferred_element_type=jnp.float32)  3.33 us
    dot_general x2, matrix products, attend_rows(): jnp.einsum('nhgd,nthd->nhgt', query_head_rows, stored_keys, preferred_ele...  2.35 us
    slice x1, local copies, waits for them, and re-layouts, body(): value_slots[step_index]  1.96 us
  transfers between devices with their start and end apart: 2, of which 0 were waited for; matrix products, arithmetic and copies ran while one was open for 23% of the time, Pallas kernels for 0%

commit v1 on v0

v1 whole, which is shorter than its diff:
```python
import functools

import jax
import jax.numpy as jnp
from jax import lax
from jax.experimental import pallas as pl
from jax.experimental.pallas import tpu as pltpu
from jax.sharding import PartitionSpec as P

HEAD_SIZE = 128
HEADS_PER_GROUP = 8
LANES = 128
MESH = pl.DeviceIdType.MESH


def kernel(
    reps,
    tps,
    per_owner,
    rank,
    x_hbm,
    q_hbm,
    k_hbm,
    v_hbm,
    ck_hbm,
    cv_hbm,
    len_hbm,
    a_hbm,
    b_hbm,
    act_hbm,
    ad_hbm,
    out_hbm,
    xbuf,
    qbuf,
    kbuf,
    vbuf,
    ckbuf,
    cvbuf,
    abuf,
    bbuf,
    len_s,
    act_s,
    ad_s,
    pbuf,
    dsend,
    down,
    drecv,
    kcb,
    vcb,
    qs,
    os,
    obuf,
    load_sem,
    out_sem,
    x_send,
    x_recv,
    p_send,
    p_recv,
    d_send,
    d_recv,
):
    rows, features = x_hbm.shape
    half = rows // len_hbm.shape[0]
    slots = k_hbm.shape[1]
    page_lanes = a_hbm.shape[0]
    width = HEADS_PER_GROUP * HEAD_SIZE
    chunks = q_hbm.shape[1] // width
    lane_groups = LANES // rank
    lane_blocks = page_lanes // LANES
    sets = pbuf.shape[1]
    scale = HEAD_SIZE ** (-0.5)
    me = lax.axis_index("rep")
    mt = lax.axis_index("tp")

    def rep_at(step):
        return lax.rem(me + step + reps, reps)

    def tp_at(step):
        return lax.rem(mt + step, tps)

    barrier = pltpu.get_barrier_semaphore()
    for k in range(1, reps):
        pl.semaphore_signal(barrier, inc=1, device_id={"rep": rep_at(k)}, device_id_type=MESH)
    for j in range(1, tps):
        pl.semaphore_signal(barrier, inc=1, device_id={"tp": tp_at(j)}, device_id_type=MESH)

    pairs = [
        (ad_hbm, ad_s),
        (x_hbm, xbuf.at[0, :, pl.ds(0, features)]),
        (act_hbm, act_s),
        (a_hbm, abuf),
        (b_hbm, bbuf),
        (q_hbm, qbuf),
        (ck_hbm, ckbuf),
        (cv_hbm, cvbuf),
        (len_hbm, len_s),
        (k_hbm, kbuf),
        (v_hbm, vbuf),
    ]
    loads = [
        pltpu.make_async_copy(src, dst, load_sem.at[i]) for i, (src, dst) in enumerate(pairs)
    ]
    for load in loads:
        load.start()
    ld_ad, ld_x, ld_act, ld_a, ld_b, ld_q, ld_ck, ld_cv, ld_len, ld_k, ld_v = loads

    row_id = lax.broadcasted_iota(jnp.int32, (rows, LANES), 0)
    lane_group = lax.broadcasted_iota(jnp.int32, (rows, LANES), 1) // rank

    ld_ad.wait()
    entry = jnp.zeros((rows, LANES), jnp.int32)
    for n in range(rows):
        entry = jnp.where(row_id == n, ad_s[n // half, n % half], entry)
    xbuf[0, :, features:] = entry.astype(jnp.float32).astype(jnp.bfloat16)
    ld_x.wait()

    pl.semaphore_wait(barrier, reps - 1 + tps - 1)

    x_copies = []
    for k in range(1, reps):
        copy = pltpu.make_async_remote_copy(
            src_ref=xbuf.at[0],
            dst_ref=xbuf.at[k],
            send_sem=x_send.at[k],
            recv_sem=x_recv.at[k],
            device_id={"rep": rep_at(k)},
            device_id_type=MESH,
        )
        copy.start()
        x_copies.append(copy)

    ld_act.wait()
    slot_of = []
    for c in range(per_owner):
        slot = jnp.zeros((rows, LANES), jnp.int32)
        for w in range(len_hbm.shape[0]):
            slot = jnp.where(row_id // half == w, act_s[w, c], slot)
        slot_of.append(slot.astype(jnp.float32))

    ld_a.wait()

    def shrink_dot(block):
        return lax.dot_general(
            block, abuf[...], (((1,), (1,)), ((), ())), preferred_element_type=jnp.float32
        )

    own_product = shrink_dot(xbuf[0, :, :features])

    ld_ck.wait()
    ld_cv.wait()
    for c in range(chunks):
        head = slice(c * HEAD_SIZE, (c + 1) * HEAD_SIZE)
        keys = ckbuf[:, head].astype(jnp.float32)
        values = cvbuf[:, head].astype(jnp.float32)
        for n in range(rows):
            place = slice(n * HEADS_PER_GROUP, (n + 1) * HEADS_PER_GROUP)
            shape = (HEADS_PER_GROUP, HEAD_SIZE)
            kcb[c, place, :] = jnp.broadcast_to(keys[n : n + 1, :], shape)
            vcb[c, place, :] = jnp.broadcast_to(values[n : n + 1, :], shape)

    for copy in x_copies:
        copy.wait_recv()
    others = shrink_dot(xbuf[1:, :, :features].reshape((reps - 1) * rows, features))

    pages = []
    packed = [jnp.zeros((rows, LANES), jnp.float32) for _ in range(sets)]
    group_f = lane_group.astype(jnp.float32)
    for k in range(reps):
        product = own_product if k == 0 else others[(k - 1) * rows : k * rows]
        entry_k = xbuf[k, :, features:].astype(jnp.float32)
        page = jnp.full((rows, LANES), -1.0, jnp.float32)
        for c in range(per_owner):
            mine = (me * per_owner + c).astype(jnp.float32)
            page = jnp.where(entry_k == mine, slot_of[c], page)
        pages.append(page)
        kept = jnp.zeros((rows, LANES), jnp.float32)
        for b in range(lane_blocks):
            kept = kept + jnp.where(
                page == group_f + float(b * lane_groups), product[:, b * LANES : (b + 1) * LANES], 0.0
            )
        turn = LANES // 2
        while turn >= rank:
            kept = kept + pltpu.roll(kept, turn, 1)
            turn //= 2
        s, g = divmod(k, lane_groups)
        packed[s] = jnp.where(lane_group == g, kept, packed[s])
    for s in range(sets):
        pbuf[0, s] = packed[s]

    p_copies = []
    for j in range(1, tps):
        copy = pltpu.make_async_remote_copy(
            src_ref=pbuf.at[0],
            dst_ref=pbuf.at[j],
            send_sem=p_send.at[j],
            recv_sem=p_recv.at[j],
            device_id={"tp": tp_at(j)},
            device_id_type=MESH,
        )
        copy.start()
        p_copies.append(copy)
    ld_b.wait()
    for copy in p_copies:
        copy.wait_recv()

    spread = []
    for k in range(reps):
        s, g = divmod(k, lane_groups)
        if g == 0:
            total = pbuf[0, s]
            for j in range(1, tps):
                total = total + pbuf[j, s]
        shrink = jnp.where(lane_group == g, total, 0.0)
        turn = LANES // 2
        while turn >= rank:
            shrink = shrink + pltpu.roll(shrink, turn, 1)
            turn //= 2
        spread.append(
            jnp.concatenate(
                [
                    jnp.where(pages[k] == group_f + float(b * lane_groups), shrink, 0.0)
                    for b in range(lane_blocks)
                ],
                axis=1,
            ).astype(jnp.bfloat16)
        )
    spread = jnp.concatenate(spread, axis=0)

    d_copies = []
    for c in range(chunks):
        delta = jnp.dot(
            spread, bbuf[:, c * width : (c + 1) * width], preferred_element_type=jnp.float32
        )
        down[c] = delta[:rows]
        here = []
        for k in range(1, reps):
            dsend[c, k] = delta[k * rows : (k + 1) * rows].astype(jnp.bfloat16)
            copy = pltpu.make_async_remote_copy(
                src_ref=dsend.at[c, k],
                dst_ref=drecv.at[c, k],
                send_sem=d_send.at[c, k],
                recv_sem=d_recv.at[c, k],
                device_id={"rep": rep_at(-k)},
                device_id_type=MESH,
            )
            copy.start()
            here.append(copy)
        d_copies.append(here)

    ld_q.wait()
    ld_len.wait()
    ld_k.wait()
    ld_v.wait()
    slot_id = lax.broadcasted_iota(jnp.int32, (HEADS_PER_GROUP, slots), 1)
    out_copies = []
    for c in range(chunks):
        cols = slice(c * width, (c + 1) * width)
        head = slice(c * HEAD_SIZE, (c + 1) * HEAD_SIZE)
        for copy in d_copies[c]:
            copy.wait_recv()
        delta = down[c]
        for k in range(1, reps):
            delta = delta + drecv[c, k].astype(jnp.float32)
        queries = (qbuf[:, cols].astype(jnp.float32) + delta).astype(jnp.bfloat16)
        queries = queries.astype(jnp.float32)
        for h in range(HEADS_PER_GROUP):
            qs[pl.ds(h, rows, stride=HEADS_PER_GROUP), :] = queries[
                :, h * HEAD_SIZE : (h + 1) * HEAD_SIZE
            ]
        scores, owns = [], []
        for n in range(rows):
            place = slice(n * HEADS_PER_GROUP, (n + 1) * HEADS_PER_GROUP)
            query = qs[place, :]
            score = lax.dot_general(
                query.astype(jnp.bfloat16),
                kbuf[n, :, head],
                (((1,), (1,)), ((), ())),
                preferred_element_type=jnp.float32,
            )
            owns.append(jnp.sum(query * kcb[c, place, :], axis=1, keepdims=True) * scale)
            length = len_s[n // half, n % half]
            scores.append(jnp.where(slot_id < length, score * scale, -jnp.inf))
        weights, own_weights, denominators = [], [], []
        for n in range(rows):
            highest = jnp.maximum(jnp.max(scores[n], axis=1, keepdims=True), owns[n])
            weight = jnp.exp(scores[n] - highest)
            own_weight = jnp.exp(owns[n] - highest)
            denominators.append(jnp.sum(weight, axis=1, keepdims=True) + own_weight)
            weights.append(weight.astype(jnp.bfloat16))
            own_weights.append(own_weight.astype(jnp.bfloat16).astype(jnp.float32))
        for n in range(rows):
            place = slice(n * HEADS_PER_GROUP, (n + 1) * HEADS_PER_GROUP)
            mixed = jnp.dot(weights[n], vbuf[n, :, head], preferred_element_type=jnp.float32)
            mixed = mixed + own_weights[n] * vcb[c, place, :]
            os[place, :] = mixed / denominators[n]
        for h in range(HEADS_PER_GROUP):
            obuf[:, c * width + h * HEAD_SIZE : c * width + (h + 1) * HEAD_SIZE] = os[
                pl.ds(h, rows, stride=HEADS_PER_GROUP), :
            ].astype(jnp.bfloat16)
        copy = pltpu.make_async_copy(
            obuf.at[:, pl.ds(c * width, width)],
            out_hbm.at[:, pl.ds(c * width, width)],
            out_sem.at[c],
        )
        copy.start()
        out_copies.append(copy)

    for copy in x_copies + p_copies:
        copy.wait_send()
    for here in d_copies:
        for copy in here:
            copy.wait_send()
    for copy in out_copies:
        copy.wait()


def body(
    reps,
    tps,
    row_states,
    q_base,
    cache_k,
    value_slots,
    current_key,
    current_value,
    cache_len,
    pool_a,
    pool_b,
    active_slots,
    row_adapter,
):
    batches, each, features = row_states.shape
    rows = batches * each
    columns = q_base.shape[2]
    slots, kv_width = cache_k.shape[2:]
    pages, rank = pool_a.shape[:2]
    width = HEADS_PER_GROUP * HEAD_SIZE
    chunks = columns // width
    sets = -(-reps * rank // LANES)
    bf16, f32 = jnp.bfloat16, jnp.float32
    dma = pltpu.SemaphoreType.DMA
    scratch = [
        pltpu.VMEM((reps, rows, features + LANES), bf16),
        pltpu.VMEM((rows, columns), bf16),
        pltpu.VMEM((rows, slots, kv_width), bf16),
        pltpu.VMEM((rows, slots, kv_width), bf16),
        pltpu.VMEM((rows, kv_width), bf16),
        pltpu.VMEM((rows, kv_width), bf16),
        pltpu.VMEM((pages * rank, features), bf16),
        pltpu.VMEM((pages * rank, columns), bf16),
        pltpu.SMEM(cache_len.shape, jnp.int32),
        pltpu.SMEM(active_slots.shape, jnp.int32),
        pltpu.SMEM((batches, each), jnp.int32),
        pltpu.VMEM((tps, sets, rows, LANES), f32),
        pltpu.VMEM((chunks, reps, rows, width), bf16),
        pltpu.VMEM((chunks, rows, width), f32),
        pltpu.VMEM((chunks, reps, rows, width), bf16),
        pltpu.VMEM((chunks, rows * HEADS_PER_GROUP, HEAD_SIZE), f32),
        pltpu.VMEM((chunks, rows * HEADS_PER_GROUP, HEAD_SIZE), f32),
        pltpu.VMEM((rows * HEADS_PER_GROUP, HEAD_SIZE), f32),
        pltpu.VMEM((rows * HEADS_PER_GROUP, HEAD_SIZE), f32),
        pltpu.VMEM((rows, columns), bf16),
        dma((11,)),
        dma((chunks,)),
        dma((reps,)),
        dma((reps,)),
        dma((tps,)),
        dma((tps,)),
        dma((chunks, reps)),
        dma((chunks, reps)),
    ]
    anywhere = pl.BlockSpec(memory_space=pl.ANY)
    out = pl.pallas_call(
        functools.partial(kernel, reps, tps, active_slots.shape[1], rank),
        out_shape=jax.ShapeDtypeStruct((rows, columns), bf16),
        in_specs=[anywhere] * 11,
        out_specs=anywhere,
        scratch_shapes=scratch,
        compiler_params=pltpu.CompilerParams(
            collective_id=0, has_side_effects=True, vmem_limit_bytes=60 * 1024 * 1024
        ),
    )(
        row_states.reshape(rows, features),
        q_base.reshape(rows, columns),
        cache_k.reshape(rows, slots, kv_width),
        value_slots.reshape(rows, slots, kv_width),
        current_key.reshape(rows, kv_width),
        current_value.reshape(rows, kv_width),
        cache_len,
        pool_a.reshape(pages * rank, features),
        pool_b.reshape(pages * rank, columns),
        active_slots,
        row_adapter.reshape(batches, each),
    )
    return out.reshape(batches, each, columns)


def solution(mesh):
    placed = (
        P(None, ("groups", "rep"), "tp"),
        P(None, ("groups", "rep"), "tp"),
        P(None, ("groups", "rep"), None, "tp"),
        P(None, ("groups", "rep"), None, "tp"),
        P(None, ("groups", "rep"), "tp"),
        P(None, ("groups", "rep"), "tp"),
        P(None, ("groups", "rep")),
        P("rep", None, "tp"),
        P("rep", None, "tp"),
        P(None, ("groups", "rep")),
        P(None, ("groups", "rep"), None),
    )
    return jax.shard_map(
        functools.partial(body, mesh.shape["rep"], mesh.shape["tp"]),
        mesh=mesh,
        in_specs=placed,
        out_specs=P(None, ("groups", "rep"), "tp"),
        check_vma=False,
    )
```

time: 97.1 us -> 25.2 us (0.26)
  blocking collectives: 53.4 us -> 0 us
  Pallas kernels: 0 us -> 23.6 us
  local copies, waits for them, and re-layouts: 17.8 us -> 1.47 us
  between operations: 13.7 us -> 0.01 us
  matrix products: 7.83 us -> 0 us
  other arithmetic: 3.97 us -> 0 us
    all_gather x2 -> x0, blocking collectives: 47.3 us -> none  [body(): page_block = lax.all_gather(owned_shrink, 'rep', axis=0, tiled=True)]
    pallas_call x0 -> x1, Pallas kernels: none -> 23.6 us  [body(): pl.pallas_call(functools.partial(kernel, reps, tps, active_slots.shape[1]...]
    unnamed x26 -> x1, local copies, waits for them, and re-layouts: 9.58 us -> 1.47 us
    dot_general x10 -> x0, matrix products: 7.83 us -> none  [the longest x2 3.33 us: body(): jnp.dot(spread, expand_flat_pages, preferred_element_type=jnp.float32)]
    psum x1 -> x0, blocking collectives: 6.13 us -> none  [body(): shrink = lax.psum(partial_value, 'tp').astype(jnp.bfloat16)]
    slice x2 -> x0, local copies, waits for them, and re-layouts: 5.53 us -> none  [the longest x1 3.57 us: body(): cache_k[step_index]]
    gather x4 -> x0, local copies, waits for them, and re-layouts: 2.24 us -> none  [the longest x2 1.13 us: body(): owned_expand = jnp.take(pool_b, active_slots[step_index], axis=0)]
    select_n x4 -> x0, other arithmetic: 1.8 us -> none  [the longest x2 1.63 us: body(): owned_expand = jnp.take(pool_b, active_slots[step_index], axis=0)]
  transfers between devices with their start and end apart: 2 -> 0, of which waited for: 0 -> 0; matrix products, arithmetic and copies ran while one was open for 23% -> 0% of each run, Pallas kernels for 0% -> 0%
where the time goes in v1:
time: 25.2 us; the launch traced here: 25.1 us
  Pallas kernels  23.6 us (94%)
  local copies, waits for them, and re-layouts  1.47 us (6%)
    pallas_call x1, Pallas kernels, body(): pl.pallas_call(functools.partial(kernel, reps, tps, active_slots.shape[1]...  23.6 us
    unnamed x1, local copies, waits for them, and re-layouts  1.47 us

profile of v1, /device:TPU:0, one launch (start us, length us, event | category | flops | bytes accessed | tf_op | source)
XLA Modules:
  0.0 25.1 jit_solution(11027137979522707139)
XLA Ops:
  0.0 23.6 %shard_map.109 = bf16[16,2048]{1,0:T(8,128)(2,1)} custom-call(bf16[16,1280]{1,0:T(8,128)(2,1)} %bitcast.16, bf16[16,2048]{1,0:T(8,128)(2,1)} %bitcast.15, bf16[16,384,256]{2,1,0:T(8,128)(2,1)} %bitcast.10, bf16[16,384,256]{2,1,0:T(8,128)(2,1)} %bitcast.11, bf16[16,256]{1,0:T(8,128)(2,1)} %bitcast.17, bf16[16,256]{1,0:T(8,128)(2,1)} %bitcast.18, ...), custom_call_target="tpu_custom_call" | custom-call | tf_op jit(solution)/shard_map/pallas_call | solution.py:373
  23.6 1.5 %copy.13 = bf16[2,8,2048]{2,1,0:T(8,128)(2,1)} copy(bf16[2,8,2048]{2,1,0:T(8,128)(2,1)} %bitcast.14) | data formatting | bytes 131072

commit v2 on v1

v2 whole, which is shorter than its diff:
```python
import functools

import jax
import jax.numpy as jnp
from jax import lax
from jax.experimental import pallas as pl
from jax.experimental.pallas import tpu as pltpu
from jax.sharding import PartitionSpec as P

HEAD_SIZE = 128
HEADS_PER_GROUP = 8
LANES = 128
MESH = pl.DeviceIdType.MESH


def kernel(
    reps,
    tps,
    per_owner,
    rank,
    x_hbm,
    q_hbm,
    k_hbm,
    v_hbm,
    ck_hbm,
    cv_hbm,
    len_hbm,
    a_hbm,
    b_hbm,
    act_hbm,
    ad_hbm,
    out_hbm,
    xbuf,
    qbuf,
    kbuf,
    vbuf,
    ckbuf,
    cvbuf,
    abuf,
    bbuf,
    len_s,
    act_s,
    ad_s,
    xs,
    pbuf,
    dsend,
    down,
    drecv,
    kcb,
    vcb,
    qs,
    os,
    wide_out,
    obuf,
    load_sem,
    out_sem,
    x_send,
    x_recv,
    p_send,
    p_recv,
    d_send,
    d_recv,
):
    rows, features = x_hbm.shape
    half = rows // len_hbm.shape[0]
    slots = k_hbm.shape[1]
    page_lanes = a_hbm.shape[0]
    width = HEADS_PER_GROUP * HEAD_SIZE
    chunks = q_hbm.shape[1] // width
    lane_groups = LANES // rank
    lane_blocks = page_lanes // LANES
    batches = len_hbm.shape[0]
    sets = pbuf.shape[2]
    fold = xbuf.shape[3]
    side_width = chunks * width // 2
    rest = features - fold
    scale = HEAD_SIZE ** (-0.5)
    last = reps - 1
    me = lax.axis_index("rep")
    mt = lax.axis_index("tp")

    def tp_at(step):
        return lax.rem(mt + step, tps)

    barrier = pltpu.get_barrier_semaphore()
    for k in range(1, reps):
        pl.semaphore_signal(
            barrier, inc=1, device_id={"rep": lax.rem(me + k, reps)}, device_id_type=MESH
        )
    for j in range(1, tps):
        pl.semaphore_signal(barrier, inc=1, device_id={"tp": tp_at(j)}, device_id_type=MESH)

    pairs = [
        (ad_hbm, ad_s),
        (x_hbm, xs),
        (act_hbm, act_s),
        (a_hbm, abuf),
        (b_hbm, bbuf),
        (q_hbm, qbuf),
        (ck_hbm, ckbuf),
        (cv_hbm, cvbuf),
        (len_hbm, len_s),
        (k_hbm, kbuf),
        (v_hbm, vbuf),
    ]
    loads = [
        pltpu.make_async_copy(src, dst, load_sem.at[i]) for i, (src, dst) in enumerate(pairs)
    ]
    for load in loads:
        load.start()
    ld_ad, ld_x, ld_act, ld_a, ld_b, ld_q, ld_ck, ld_cv, ld_len, ld_k, ld_v = loads

    row_id = lax.broadcasted_iota(jnp.int32, (rows, LANES), 0)
    lane_group = lax.broadcasted_iota(jnp.int32, (half, LANES), 1) // rank

    ld_ad.wait()
    entry = jnp.zeros((rows, LANES), jnp.int32)
    for n in range(rows):
        entry = jnp.where(row_id == n, ad_s[n // half, n % half], entry)
    entry = entry.astype(jnp.float32)
    ld_x.wait()
    for w in range(batches):
        mine = slice(w * half, (w + 1) * half)
        states = xs[...].astype(jnp.float32)[mine]
        below = [states[:, fold:], entry[mine]]
        if rest + LANES < fold:
            below.append(jnp.zeros((half, fold - rest - LANES), jnp.float32))
        folded = jnp.concatenate([states[:, :fold], jnp.concatenate(below, axis=1)], axis=0)
        xbuf[w, me] = folded.astype(jnp.bfloat16)

    pl.semaphore_wait(barrier, last + tps - 1)

    def reaches(side, step):
        return me + step <= last if side > 0 else me - step >= 0

    def arrives(side, step):
        return me - step >= 0 if side > 0 else me + step <= last

    def row_copy(w, side, step, peer, slot):
        return pltpu.make_async_remote_copy(
            src_ref=xbuf.at[w, slot],
            dst_ref=xbuf.at[w, slot],
            send_sem=x_send.at[w, (side + 1) // 2, step],
            recv_sem=x_recv.at[w, (side + 1) // 2, step],
            device_id={"rep": peer},
            device_id_type=MESH,
        )

    for w in range(batches):
        for step in range(last, 0, -1):
            for side in (1, -1):

                @pl.when(reaches(side, step))
                def _():
                    row_copy(w, side, step, me + side * step, me).start()

    for w in range(batches):
        drecv[w, me] = jnp.zeros((rows, side_width), jnp.bfloat16)

    ld_act.wait()
    ld_a.wait()

    def shrink_dot(block):
        return lax.dot_general(
            block, abuf[...], (((1,), (1,)), ((), ())), preferred_element_type=jnp.float32
        )

    ld_ck.wait()
    ld_cv.wait()
    for c in range(chunks):
        head = slice(c * HEAD_SIZE, (c + 1) * HEAD_SIZE)
        keys = ckbuf[:, head].astype(jnp.float32)
        values = cvbuf[:, head].astype(jnp.float32)
        for n in range(rows):
            place = slice(n * HEADS_PER_GROUP, (n + 1) * HEADS_PER_GROUP)
            shape = (HEADS_PER_GROUP, HEAD_SIZE)
            kcb[c, place, :] = jnp.broadcast_to(keys[n : n + 1, :], shape)
            vcb[c, place, :] = jnp.broadcast_to(values[n : n + 1, :], shape)

    group_f = lane_group.astype(jnp.float32)
    ld_b.wait()

    def shrink_part(w):
        for step in range(1, reps):
            for side in (1, -1):

                @pl.when(arrives(side, step))
                def _():
                    row_copy(w, side, step, me - side * step, me - side * step).wait_recv()

        states, entries = [], []
        for k in range(reps):
            folded = xbuf[w, k].astype(jnp.float32)
            states.append(jnp.concatenate([folded[:half], folded[half:, :rest]], axis=1))
            entries.append(folded[half:, rest : rest + LANES])
        products = shrink_dot(jnp.concatenate(states, axis=0).astype(jnp.bfloat16))
        pages = []
        packed = [jnp.zeros((half, LANES), jnp.float32) for _ in range(sets)]
        for k in range(reps):
            product = products[k * half : (k + 1) * half]
            page = jnp.full((half, LANES), -1.0, jnp.float32)
            for c in range(per_owner):
                mine = (me * per_owner + c).astype(jnp.float32)
                page = jnp.where(entries[k] == mine, act_s[w, c].astype(jnp.float32), page)
            pages.append(page)
            kept = jnp.zeros((half, LANES), jnp.float32)
            for b in range(lane_blocks):
                kept = kept + jnp.where(
                    page == group_f + float(b * lane_groups),
                    product[:, b * LANES : (b + 1) * LANES],
                    0.0,
                )
            turn = LANES // 2
            while turn >= rank:
                kept = kept + pltpu.roll(kept, turn, 1)
                turn //= 2
            s, g = divmod(k, lane_groups)
            packed[s] = jnp.where(lane_group == g, kept, packed[s])
        for s in range(sets):
            pbuf[w, 0, s] = packed[s]
        copies = []
        for j in range(1, tps):
            copy = pltpu.make_async_remote_copy(
                src_ref=pbuf.at[w, 0],
                dst_ref=pbuf.at[w, j],
                send_sem=p_send.at[w, j],
                recv_sem=p_recv.at[w, j],
                device_id={"tp": tp_at(j)},
                device_id_type=MESH,
            )
            copy.start()
            copies.append(copy)
        return pages, copies

    def delta_copy(w, side, step, peer, slot):
        return pltpu.make_async_remote_copy(
            src_ref=dsend.at[w, peer],
            dst_ref=drecv.at[w, slot],
            send_sem=d_send.at[w, (side + 1) // 2, step],
            recv_sem=d_recv.at[w, (side + 1) // 2, step],
            device_id={"rep": peer},
            device_id_type=MESH,
        )

    def expand_part(w, pages, copies):
        for copy in copies:
            copy.wait_recv()
        spread = []
        for k in range(reps):
            s, g = divmod(k, lane_groups)
            if g == 0:
                total = pbuf[w, 0, s]
                for j in range(1, tps):
                    total = total + pbuf[w, j, s]
            shrink = jnp.where(lane_group == g, total, 0.0)
            turn = LANES // 2
            while turn >= rank:
                shrink = shrink + pltpu.roll(shrink, turn, 1)
                turn //= 2
            spread.append(
                jnp.concatenate(
                    [
                        jnp.where(pages[k] == group_f + float(b * lane_groups), shrink, 0.0)
                        for b in range(lane_blocks)
                    ],
                    axis=1,
                )
            )
        spread = jnp.concatenate(spread, axis=0).astype(jnp.bfloat16)
        sides = [
            jnp.dot(
                spread,
                bbuf[:, i * side_width : (i + 1) * side_width],
                preferred_element_type=jnp.float32,
            )
            for i in range(2)
        ]
        for k in range(reps):
            block = jnp.concatenate([side[k * half : (k + 1) * half] for side in sides], axis=0)
            down[w, k] = block
            dsend[w, k] = block.astype(jnp.bfloat16)
        for step in range(last, 0, -1):
            for side in (1, -1):

                @pl.when(reaches(side, step))
                def _():
                    delta_copy(w, side, step, me + side * step, me).start()

    shrunk = [shrink_part(w) for w in range(batches)]
    for w in range(batches):
        expand_part(w, *shrunk[w])

    ld_q.wait()
    ld_len.wait()
    ld_k.wait()
    ld_v.wait()
    slot_id = lax.broadcasted_iota(jnp.int32, (HEADS_PER_GROUP, slots), 1)
    for w in range(batches):
        for step in range(1, reps):
            for side in (1, -1):

                @pl.when(arrives(side, step))
                def _():
                    delta_copy(w, side, step, me - side * step, me - side * step).wait_recv()

        delta = down[w, me]
        for k in range(reps):
            delta = delta + drecv[w, k].astype(jnp.float32)
        delta = jnp.concatenate([delta[:half], delta[half:]], axis=1)
        base = qbuf[...].astype(jnp.float32)[w * half : (w + 1) * half]
        queries = (base + delta).astype(jnp.bfloat16).astype(jnp.float32)
        pairs = [(c, n) for c in range(chunks) for n in range(half)]

        def place(c, n):
            start = (c * half + n) * HEADS_PER_GROUP
            return slice(start, start + HEADS_PER_GROUP)

        def wide(n):
            start = (w * half + n) * HEADS_PER_GROUP
            return slice(start, start + HEADS_PER_GROUP)

        for c in range(chunks):
            for h in range(HEADS_PER_GROUP):
                first = c * width + h * HEAD_SIZE
                qs[pl.ds(c * half * HEADS_PER_GROUP + h, half, stride=HEADS_PER_GROUP), :] = queries[
                    :, first : first + HEAD_SIZE
                ]
        scores, owns = [], []
        for c, n in pairs:
            query = qs[place(c, n), :]
            score = lax.dot_general(
                query.astype(jnp.bfloat16),
                kbuf[w * half + n, :, c * HEAD_SIZE : (c + 1) * HEAD_SIZE],
                (((1,), (1,)), ((), ())),
                preferred_element_type=jnp.float32,
            )
            owns.append(jnp.sum(query * kcb[c, wide(n), :], axis=1, keepdims=True) * scale)
            scores.append(jnp.where(slot_id < len_s[w, n], score * scale, -jnp.inf))
        weights, own_weights, denominators = [], [], []
        for score, own in zip(scores, owns):
            highest = jnp.maximum(jnp.max(score, axis=1, keepdims=True), own)
            weight = jnp.exp(score - highest)
            own_weight = jnp.exp(own - highest)
            denominators.append(jnp.sum(weight, axis=1, keepdims=True) + own_weight)
            weights.append(weight.astype(jnp.bfloat16))
            own_weights.append(own_weight.astype(jnp.bfloat16).astype(jnp.float32))
        for i, (c, n) in enumerate(pairs):
            mixed = jnp.dot(
                weights[i],
                vbuf[w * half + n, :, c * HEAD_SIZE : (c + 1) * HEAD_SIZE],
                preferred_element_type=jnp.float32,
            )
            mixed = mixed + own_weights[i] * vcb[c, wide(n), :]
            os[place(c, n), :] = mixed / denominators[i]
        for c in range(chunks):
            for h in range(HEADS_PER_GROUP):
                first = c * width + h * HEAD_SIZE
                wide_out[w * half : (w + 1) * half, first : first + HEAD_SIZE] = os[
                    pl.ds(c * half * HEADS_PER_GROUP + h, half, stride=HEADS_PER_GROUP), :
                ]
    obuf[...] = wide_out[...].astype(jnp.bfloat16)
    out_copy = pltpu.make_async_copy(obuf, out_hbm, out_sem)
    out_copy.start()

    for _, copies in shrunk:
        for copy in copies:
            copy.wait_send()
    for step in range(1, reps):
        for side in (1, -1):

            @pl.when(reaches(side, step))
            def _():
                for w in range(batches):
                    row_copy(w, side, step, me + side * step, me).wait_send()
                    delta_copy(w, side, step, me + side * step, me).wait_send()

    out_copy.wait()


def body(
    reps,
    tps,
    row_states,
    q_base,
    cache_k,
    value_slots,
    current_key,
    current_value,
    cache_len,
    pool_a,
    pool_b,
    active_slots,
    row_adapter,
):
    batches, each, features = row_states.shape
    rows = batches * each
    columns = q_base.shape[2]
    slots, kv_width = cache_k.shape[2:]
    pages, rank = pool_a.shape[:2]
    width = HEADS_PER_GROUP * HEAD_SIZE
    chunks = columns // width
    sets = -(-reps * rank // LANES)
    fold = (features + 2 * LANES) // (2 * LANES) * LANES
    bf16, f32 = jnp.bfloat16, jnp.float32
    dma = pltpu.SemaphoreType.DMA
    scratch = [
        pltpu.VMEM((batches, reps, rows, fold), bf16),
        pltpu.VMEM((rows, columns), bf16),
        pltpu.VMEM((rows, slots, kv_width), bf16),
        pltpu.VMEM((rows, slots, kv_width), bf16),
        pltpu.VMEM((rows, kv_width), bf16),
        pltpu.VMEM((rows, kv_width), bf16),
        pltpu.VMEM((pages * rank, features), bf16),
        pltpu.VMEM((pages * rank, columns), bf16),
        pltpu.SMEM(cache_len.shape, jnp.int32),
        pltpu.SMEM(active_slots.shape, jnp.int32),
        pltpu.SMEM((batches, each), jnp.int32),
        pltpu.VMEM((rows, features), bf16),
        pltpu.VMEM((batches, tps, sets, each, LANES), f32),
        pltpu.VMEM((batches, reps, rows, columns // 2), bf16),
        pltpu.VMEM((batches, reps, rows, columns // 2), f32),
        pltpu.VMEM((batches, reps, rows, columns // 2), bf16),
        pltpu.VMEM((chunks, rows * HEADS_PER_GROUP, HEAD_SIZE), f32),
        pltpu.VMEM((chunks, rows * HEADS_PER_GROUP, HEAD_SIZE), f32),
        pltpu.VMEM((chunks * each * HEADS_PER_GROUP, HEAD_SIZE), f32),
        pltpu.VMEM((chunks * each * HEADS_PER_GROUP, HEAD_SIZE), f32),
        pltpu.VMEM((rows, columns), f32),
        pltpu.VMEM((rows, columns), bf16),
        dma((11,)),
        dma,
        dma((batches, 2, reps)),
        dma((batches, 2, reps)),
        dma((batches, tps)),
        dma((batches, tps)),
        dma((batches, 2, reps)),
        dma((batches, 2, reps)),
    ]
    anywhere = pl.BlockSpec(memory_space=pl.ANY)
    out = pl.pallas_call(
        functools.partial(kernel, reps, tps, active_slots.shape[1], rank),
        out_shape=jax.ShapeDtypeStruct((rows, columns), bf16),
        in_specs=[anywhere] * 11,
        out_specs=anywhere,
        scratch_shapes=scratch,
        compiler_params=pltpu.CompilerParams(
            collective_id=0, has_side_effects=True, vmem_limit_bytes=60 * 1024 * 1024
        ),
    )(
        row_states.reshape(rows, features),
        q_base.reshape(rows, columns),
        cache_k.reshape(rows, slots, kv_width),
        value_slots.reshape(rows, slots, kv_width),
        current_key.reshape(rows, kv_width),
        current_value.reshape(rows, kv_width),
        cache_len,
        pool_a.reshape(pages * rank, features),
        pool_b.reshape(pages * rank, columns),
        active_slots,
        row_adapter.reshape(batches, each),
    )
    return out.reshape(batches, each, columns)


def solution(mesh):
    placed = (
        P(None, ("groups", "rep"), "tp"),
        P(None, ("groups", "rep"), "tp"),
        P(None, ("groups", "rep"), None, "tp"),
        P(None, ("groups", "rep"), None, "tp"),
        P(None, ("groups", "rep"), "tp"),
        P(None, ("groups", "rep"), "tp"),
        P(None, ("groups", "rep")),
        P("rep", None, "tp"),
        P("rep", None, "tp"),
        P(None, ("groups", "rep")),
        P(None, ("groups", "rep"), None),
    )
    return jax.shard_map(
        functools.partial(body, mesh.shape["rep"], mesh.shape["tp"]),
        mesh=mesh,
        in_specs=placed,
        out_specs=P(None, ("groups", "rep"), "tp"),
        check_vma=False,
    )
```

time: 25.2 us -> 25 us (level)
  Pallas kernels: 23.6 us -> 23.3 us
where the time goes in v2:
time: 25 us; the launch traced here: 24.8 us
  Pallas kernels  23.3 us (93%)
  local copies, waits for them, and re-layouts  1.47 us (6%)
    pallas_call x1, Pallas kernels, body(): pl.pallas_call(functools.partial(kernel, reps, tps, active_slots.shape[1]...  23.3 us
    unnamed x1, local copies, waits for them, and re-layouts  1.47 us

profile of v2, /device:TPU:0, one launch (start us, length us, event | category | flops | bytes accessed | tf_op | source)
XLA Modules:
  0.0 24.8 jit_solution(16117778055204536613)
XLA Ops:
  0.0 23.3 %shard_map.109 = bf16[16,2048]{1,0:T(8,128)(2,1)} custom-call(bf16[16,1280]{1,0:T(8,128)(2,1)} %bitcast.16, bf16[16,2048]{1,0:T(8,128)(2,1)} %bitcast.15, bf16[16,384,256]{2,1,0:T(8,128)(2,1)} %bitcast.10, bf16[16,384,256]{2,1,0:T(8,128)(2,1)} %bitcast.11, bf16[16,256]{1,0:T(8,128)(2,1)} %bitcast.17, bf16[16,256]{1,0:T(8,128)(2,1)} %bitcast.18, ...), custom_call_target="tpu_custom_call" | custom-call | tf_op jit(solution)/shard_map/pallas_call | solution.py:439
  23.3 1.5 %copy.13 = bf16[2,8,2048]{2,1,0:T(8,128)(2,1)} copy(bf16[2,8,2048]{2,1,0:T(8,128)(2,1)} %bitcast.14) | data formatting | bytes 131072

commit v3 on v2

--- a/solution.py
+++ b/solution.py
@@ -342,14 +342,22 @@
             weight = jnp.exp(score - highest)
             own_weight = jnp.exp(own - highest)
             denominators.append(jnp.sum(weight, axis=1, keepdims=True) + own_weight)
-            weights.append(weight.astype(jnp.bfloat16))
+            weights.append(weight)
             own_weights.append(own_weight.astype(jnp.bfloat16).astype(jnp.float32))
-        for i, (c, n) in enumerate(pairs):
-            mixed = jnp.dot(
-                weights[i],
-                vbuf[w * half + n, :, c * HEAD_SIZE : (c + 1) * HEAD_SIZE],
+        joint = [
+            jnp.dot(
+                jnp.concatenate([weights[c * half + n] for c in range(chunks)], axis=0).astype(
+                    jnp.bfloat16
+                ),
+                vbuf[w * half + n],
                 preferred_element_type=jnp.float32,
             )
+            for n in range(half)
+        ]
+        for i, (c, n) in enumerate(pairs):
+            mixed = joint[n][
+                c * HEADS_PER_GROUP : (c + 1) * HEADS_PER_GROUP, c * HEAD_SIZE : (c + 1) * HEAD_SIZE
+            ]
             mixed = mixed + own_weights[i] * vcb[c, wide(n), :]
             os[place(c, n), :] = mixed / denominators[i]
         for c in range(chunks):

time: 25 us -> 24.9 us (level)
  no operation moved by 1% of the time
where the time goes in v3:
time: 24.9 us; the launch traced here: 24.7 us
  Pallas kernels  23.3 us (94%)
  local copies, waits for them, and re-layouts  1.47 us (6%)
    pallas_call x1, Pallas kernels, body(): pl.pallas_call(functools.partial(kernel, reps, tps, active_slots.shape[1]...  23.3 us
    unnamed x1, local copies, waits for them, and re-layouts  1.47 us

profile of v3, /device:TPU:0, one launch (start us, length us, event | category | flops | bytes accessed | tf_op | source)
XLA Modules:
  0.0 24.7 jit_solution(4378471839522102175)
XLA Ops:
  0.0 23.3 %shard_map.109 = bf16[16,2048]{1,0:T(8,128)(2,1)} custom-call(bf16[16,1280]{1,0:T(8,128)(2,1)} %bitcast.16, bf16[16,2048]{1,0:T(8,128)(2,1)} %bitcast.15, bf16[16,384,256]{2,1,0:T(8,128)(2,1)} %bitcast.10, bf16[16,384,256]{2,1,0:T(8,128)(2,1)} %bitcast.11, bf16[16,256]{1,0:T(8,128)(2,1)} %bitcast.17, bf16[16,256]{1,0:T(8,128)(2,1)} %bitcast.18, ...), custom_call_target="tpu_custom_call" | custom-call | tf_op jit(solution)/shard_map/pallas_call | solution.py:447
  23.3 1.5 %copy.13 = bf16[2,8,2048]{2,1,0:T(8,128)(2,1)} copy(bf16[2,8,2048]{2,1,0:T(8,128)(2,1)} %bitcast.14) | data formatting | bytes 131072
